TPU v7x, 512 devices: a whole 4x4x16 slice. The times are simulated.
512 devices in a mesh: section: 4 (over y), row: 16 (over z), col: 8 (over x, core).
Axes of the slice: x: 4, y: 4, z: 16, core: 2. Of those that a mesh axis runs over, the one named last changes fastest.
Arguments:
- grad_out: bfloat16 [4, 320, 6144], P('section', 'col', 'row'), may hold values from -34 to 34
- pre_act: bfloat16 [4, 320, 24576], P('section', 'row', 'col'), may hold values from -36 to 36
- w_down: bfloat16 [4, 24576, 6144], P('section', 'col', 'row'), may hold values from -0.0390625 to 0.0390625
Outputs:
- grad_pre: bfloat16 [4, 320, 24576], P('section', 'row', 'col')
- grad_weight: bfloat16 [4, 24576, 6144], P('section', 'col', 'row')
All inputs are finite; a program needn't handle non-finite values.
Results may differ from a plain program's by a relative error of at most 0.0034.
Values may be sent and summed in bfloat16 or wider, within the bound.
A program may use at most 64 MiB of HBM per device.

v0:
```python
import math

import jax
import jax.numpy as jnp
from jax import lax
from jax.sharding import PartitionSpec as P

D = 6144
FFW = 24576


gelu_coef = 0.7978845608028654
cubic_coef = 0.044715
target_rms = 0.5
tiny_eps = 1e-06


def gelu_parts(field):
    tanh_val = jnp.tanh(gelu_coef * (field + cubic_coef * field * field * field))
    values = 0.5 * field * (1.0 + tanh_val)
    slopes = 0.5 * (1.0 + tanh_val) + 0.5 * field * (1.0 - tanh_val * tanh_val) * gelu_coef * (
        1.0 + 3.0 * cubic_coef * field * field
    )
    return (values, slopes)


def on_device(grad_out, pre_act, w_down):
    grad_block = grad_out[0]
    pre_acts = pre_act[0]
    weights = w_down[0]
    grad_rows = lax.all_gather(grad_block, "col", axis=0, tiled=True)
    values, slopes = gelu_parts(pre_acts.astype(jnp.float32))
    row_block = grad_rows
    act_grad = lax.psum_scatter(
        lax.dot_general(
            row_block, weights, (((1,), (1,)), ((), ())), preferred_element_type=jnp.float32
        ),
        "row",
        scatter_dimension=0,
        tiled=True,
    )
    grad_pre = (act_grad * slopes).astype(jnp.bfloat16)
    row_block = grad_rows
    weight_grad = lax.dot_general(
        lax.all_gather(values.astype(jnp.bfloat16), "row", axis=0, tiled=True),
        row_block,
        (((0,), (0,)), ((), ())),
        preferred_element_type=jnp.float32,
    )
    sum_squares = lax.psum(jnp.sum(weight_grad * weight_grad), ("section", "row", "col"))
    weight_grad, sum_squares = (weight_grad, sum_squares)
    norm_target = target_rms * math.sqrt(float(lax.axis_size("section") * FFW * D))
    factor = norm_target / jnp.sqrt(sum_squares + tiny_eps)
    grad_weight = (weight_grad * factor).astype(jnp.bfloat16)
    return (grad_pre[None], grad_weight[None])


def solution(mesh):
    in_specs = (P("section", "col", "row"), P("section", "row", "col"), P("section", "col", "row"))
    out_specs = (P("section", "row", "col"), P("section", "col", "row"))
    return jax.shard_map(
        on_device, mesh=mesh, in_specs=in_specs, out_specs=out_specs, check_vma=False
    )
```

profile of v0, /device:TPU:1, one launch (start us, length us, event | category | flops | bytes accessed | tf_op | source)
XLA Modules:
  0.0 331.7 jit_solution(458032746624342053)
XLA Ops:
  7.2 0.0 copy-start
  7.2 0.0 all-gather.4.cloned.1.call-start
  7.2 19.9 %all-gather = bf16[1,320,384]{2,1,0:T(8,128)(2,1)S(1)} all-gather(bf16[1,40,384]{2,1,0:T(8,128)(2,1)} %param.3), channel_id=2, replica_groups=mesh['section'=4,'row'=16,'col'=8] {'col'}, dimensions={1}, use_global_device_ids=true | all-gather | bytes 276480 | tf_op jit(solution)/shard_map/all_gather | solution.py:31
  27.1 0.0 copy-done
  27.1 3.1 fusion.2
  30.2 58.9 %fusion = f32[24,3072]{1,0:T(8,128)S(1)} fusion(f32[320,3072]{1,0:T(8,128)} %fusion.2), kind=kCustom, calls=%all-reduce-scatter | all-reduce-scatter fusion | flops 1179649 | bytes 4229120
  89.1 1.3 collective-permute-start.1
  90.5 2.1 collective-permute-start
  92.6 0.7 slice
  93.2 4.4 %collective-permute-start.2 = (f32[12,3072]{1,0:T(8,128)}, f32[12,3072]{1,0:T(8,128)}, u32[]{:S(2)}, u32[]{:S(2)}) collective-permute-start(f32[12,3072]{1,0:T(8,128)} %slice), channel_id=1, source_target_pairs={{0,24},{8,32},{16,40},{24,48},{32,56},{40,64},{48,72},{56,80},{64,... | collective-permute-start | bytes 442376
  97.7 1.3 dynamic-slice.4
  99.6 6.9 %collective-permute-done.2 = f32[12,3072]{1,0:T(8,128)} collective-permute-done((f32[12,3072]{1,0:T(8,128)}, f32[12,3072]{1,0:T(8,128)}, u32[]{:S(2)}, u32[]{:S(2)}) %collective-permute-start.2) | collective-permute-done | bytes 147488
  106.5 0.0 collective-permute-done.1
  106.5 0.0 collective-permute-done
  106.5 10.4 %concatenate = f32[84,3072]{1,0:T(8,128)} concatenate(f32[12,3072]{1,0:T(8,128)} %collective-permute-done.2, f32[24,3072]{1,0:T(8,128)S(1)} %collective-permute-done.1, f32[24,3072]{1,0:T(8,128)S(1)} %collective-permute-done, f32[24,3072]{1,0:T(8,128)S(1)} %fusion), dimensions={0} | concatenate | bytes 2064384
  116.8 2.0 fusion.18
  118.9 0.0 all-gather.4.cloned.1.call-update
  118.9 80.7 %all-gather.4.cloned.1.call-done = bf16[16,20,3072]{2,1,0:T(8,128)(2,1)} async-done(((bf16[1,20,3072]{2,1,0:T(8,128)(2,1)}), bf16[16,20,3072]{2,1,0:T(8,128)(2,1)}) %all-gather.4.cloned.1.call-update) | async-done | bytes 1966096 | tf_op jit(solution)/shard_map/all_gather | solution.py:45
  199.6 3.9 %reshape.9 = bf16[320,3072]{1,0:T(8,128)(2,1)} reshape(bf16[16,20,3072]{2,1,0:T(8,128)(2,1)} %all-gather.4.cloned.1.call-done) | data formatting | bytes 3932160
  203.5 6.1 %multiply_reduce_fusion = (f32[]{:T(128)}, f32[3072,384]{1,0:T(8,128)}) fusion(bf16[320,3072]{1,0:T(8,128)(2,1)} %reshape.9, bf16[1,320,384]{2,1,0:T(8,128)(2,1)S(1)} %all-gather), kind=kOutput, calls=%fused_computation.1 | convolution fusion | flops 757334016 | bytes 6930436 | tf_op jit(solution)/shard_map/dot_general | solution.py:44
  209.6 110.4 %psum.7 = f32[]{:T(128)} all-reduce(f32[]{:T(128)} %get-tuple-element.4), channel_id=1, replica_groups=mesh['section'=4,'row'=16,'col'=8] {'section','row','col'}, use_global_device_ids=true, to_apply=%region_2.0 | all-reduce | flops 1 | bytes 8 | tf_op jit(solution)/shard_map/psum | solution.py:50
  320.8 4.1 %fusion.1 = bf16[1,3072,384]{2,1,0:T(8,128)(2,1)} fusion(f32[3072,384]{1,0:T(8,128)} %get-tuple-element.5, f32[]{:T(128)S(6)} %div.3), kind=kLoop, calls=%fused_computation.2 | loop fusion | flops 2359296 | bytes 7077892 | tf_op jit(solution)/shard_map/broadcast_in_dim | solution.py:55
Async XLA Ops:
  7.2 19.9 %copy-start = (bf16[1,3072,384]{2,1,0:T(8,128)(2,1)S(1)}, bf16[1,3072,384]{2,1,0:T(8,128)(2,1)}, u32[]{:S(2)}) copy-start(bf16[1,3072,384]{2,1,0:T(8,128)(2,1)} %param.5) | copy-start | bytes 7077892
  7.2 192.4 %all-gather.4.cloned.1.call-start = ((), (), s32[]{:S(2)}) async-start(), calls=%async_computation | async-start | bytes 2506752 | tf_op jit(solution)/shard_map/all_gather | solution.py:45
  89.1 17.3 %collective-permute-start.1 = (f32[24,3072]{1,0:T(8,128)S(1)}, f32[24,3072]{1,0:T(8,128)S(1)}, u32[]{:S(2)}, u32[]{:S(2)}) collective-permute-start(f32[24,3072]{1,0:T(8,128)S(1)} %fusion), channel_id=1, source_target_pairs={{0,16},{8,24},{16,32},{24,40},{32,48},{40,56},{48,64},{56,72},{64,... | collective-permute-start | bytes 884744
  90.5 16.0 %collective-permute-start = (f32[24,3072]{1,0:T(8,128)S(1)}, f32[24,3072]{1,0:T(8,128)S(1)}, u32[]{:S(2)}, u32[]{:S(2)}) collective-permute-start(f32[24,3072]{1,0:T(8,128)S(1)} %fusion), channel_id=1, source_target_pairs={{0,8},{8,16},{16,24},{24,32},{32,40},{40,48},{48,56},{56,64},{64,7... | collective-permute-start | bytes 884744
  93.2 13.2 %collective-permute-start.2 = (f32[12,3072]{1,0:T(8,128)}, f32[12,3072]{1,0:T(8,128)}, u32[]{:S(2)}, u32[]{:S(2)}) collective-permute-start(f32[12,3072]{1,0:T(8,128)} %slice), channel_id=1, source_target_pairs={{0,24},{8,32},{16,40},{24,48},{32,56},{40,64},{48,72},{56,80},{64,... | collective-permute-start | bytes 442376
Sparse Core Ops, SparseCore 0:
  119.0 80.5 all-gather.3
where the time goes:
time: 333 us; the launch traced here: 332 us
  blocking collectives  189 us (57%)
  waiting for transfers between devices  87.6 us (26%)
  local copies, waits for them, and re-layouts  16.3 us (5%)
  between operations  15.4 us (5%)
  matrix products  9.23 us (3%)
  starting transfers between devices  7.86 us (2%)
  other arithmetic  6.12 us (2%)
    psum x1, blocking collectives, on_device(): lax.psum(jnp.sum(weight_grad * weight_grad), ('section', 'row', 'col'))  110 us
    all_gather x1, waiting for transfers between devices, on_device(): lax.all_gather(values.astype(jnp.bfloat16), 'row', axis=0, tiled=True)  80.7 us
    unnamed x1, blocking collectives  58.9 us
    all_gather x1, blocking collectives, on_device(): grad_rows = lax.all_gather(grad_block, 'col', axis=0, tiled=True)  19.9 us
    unnamed x6, local copies, waits for them, and re-layouts  16.3 us
    unnamed x3, starting transfers between devices  7.83 us
    unnamed x4, waiting for transfers between devices  6.89 us
  transfers between devices with their start and end apart: 4, of which 2 were waited for; matrix products, arithmetic and copies ran while one was open for 1% of the time, Pallas kernels for 0%

commit v1 on v0

v1 whole, which is shorter than its diff:
```python
import functools
import math

import jax
import jax.numpy as jnp
from jax import lax
from jax.experimental import pallas as pl
from jax.experimental.pallas import tpu as pltpu
from jax.sharding import PartitionSpec as P

MESH = pl.DeviceIdType.MESH

gelu_coef = 0.7978845608028654
cubic_coef = 0.044715
target_rms = 0.5
tiny_eps = 1e-06

ROWS = 16
QUARTERS = 4
PARTS = 2
LAG = 4


def gelu_parts(field):
    tanh_val = jnp.tanh(gelu_coef * (field + cubic_coef * field * field * field))
    values = 0.5 * field * (1.0 + tanh_val)
    slopes = 0.5 * (1.0 + tanh_val) + 0.5 * field * (1.0 - tanh_val * tanh_val) * gelu_coef * (
        1.0 + 3.0 * cubic_coef * field * field
    )
    return (values, slopes)


def encode(v):
    return (v * jnp.abs(v) * (v * v)).astype(jnp.bfloat16)


def decode(code):
    y = code.astype(jnp.float32)
    size = jnp.abs(y)
    root = jnp.sqrt(jnp.sqrt(size))
    return jnp.where(y < 0.0, -root, root)


def kernel(
    n_row, n_col, n_sec, norm_target,
    g_ref, pre_ref, w_hbm, gp_ref, gw_hbm,
    w_buf, acts, packed, slopes_buf, gbuf, gmain, gtail, part, raw, out_buf,
    rs_out, rs_in, peak, ss_row, ss_col, ss_sec,
    w_sem, out_sem, ag_send, ag_recv, rs_send, rs_recv, g_send, g_recv,
    peak_send, peak_recv, ssr_send, ssr_recv, ssc_send, ssc_recv, sss_send, sss_recv,
):
    f32, bf16 = jnp.float32, jnp.bfloat16
    row, col, sec = lax.axis_index("row"), lax.axis_index("col"), lax.axis_index("section")
    hidden, feats = w_buf.shape
    quarter = hidden // QUARTERS
    width = hidden + quarter
    pw = width // PARTS
    extra = pre_ref.shape[1] - ROWS
    half = n_row // 2

    def peer(axis, index, size, d):
        return {axis: lax.rem(index + d, size)}

    row_peers = [peer("row", row, n_row, d) for d in range(n_row)]
    col_peers = [peer("col", col, n_col, d) for d in range(n_col)]
    sec_peers = [peer("section", sec, n_sec, d) for d in range(n_sec)]

    barrier = pltpu.get_barrier_semaphore()
    others = row_peers[1:] + col_peers[1:] + sec_peers[1:]
    for device in others:
        pl.semaphore_signal(barrier, inc=1, device_id=device, device_id_type=MESH)
    w_copy = pltpu.make_async_copy(w_hbm.at[0], w_buf, w_sem)
    w_copy.start()

    pre = pre_ref[0].astype(f32)
    packed[:, pl.ds(0, hidden)] = pre[:ROWS]
    for q in range(QUARTERS):
        packed[pl.ds(q * extra, extra), pl.ds(hidden, quarter)] = pre[ROWS:, q * quarter:(q + 1) * quarter]
    values, slopes = gelu_parts(packed[...])
    acts[0] = values.astype(bf16)
    slopes_buf[...] = slopes

    g = g_ref[0].astype(f32)
    for b in range(2):
        base = b * (ROWS + extra)
        gbuf[0, 0, b] = g[base:base + ROWS].astype(bf16)
        last = g[base + ROWS:base + ROWS + extra]
        gbuf[0, 1, b] = jnp.concatenate([last] * QUARTERS, axis=0).astype(bf16)

    pl.semaphore_wait(barrier, len(others))

    def hops(way, p):
        return half if (way + p) % 2 == 0 else half - 1

    def lanes(p):
        return pl.ds(p * pw, pw)

    def toward(way):
        return row_peers[1] if way == 0 else row_peers[n_row - 1]

    def ag_copy(way, p, h):
        src = (h - 1) if way == 0 else (n_row - h + 1) % n_row
        dst = h if way == 0 else n_row - h
        return pltpu.make_async_remote_copy(
            src_ref=acts.at[src, :, lanes(p)],
            dst_ref=acts.at[dst, :, lanes(p)],
            send_sem=ag_send.at[way, p, h - 1],
            recv_sem=ag_recv.at[way, p, h - 1],
            device_id=toward(way),
            device_id_type=MESH,
        )

    def rs_copy(way, p, k):
        return pltpu.make_async_remote_copy(
            src_ref=rs_out.at[way, p, k - 1],
            dst_ref=rs_in.at[way, p, k - 1],
            send_sem=rs_send.at[way, p, k - 1],
            recv_sem=rs_recv.at[way, p, k - 1],
            device_id=toward(way),
            device_id_type=MESH,
        )

    def spread(buf, send, recv, peers):
        return [
            pltpu.make_async_remote_copy(
                src_ref=buf.at[0], dst_ref=buf.at[d], send_sem=send.at[d], recv_sem=recv.at[d],
                device_id=peers[d], device_id_type=MESH,
            )
            for d in range(1, len(peers))
        ]

    flows = [(way, p) for p in range(PARTS) for way in range(2)]

    def ag_step(h):
        for way, p in flows:
            if h >= 2 and h - 1 <= hops(way, p):
                ag_copy(way, p, h - 1).wait_recv()
            if h <= hops(way, p):
                ag_copy(way, p, h).start()

    ag_step(1)
    g_copies = spread(gbuf, g_send, g_recv, col_peers)
    for c in g_copies:
        c.start()
    ag_step(2)
    w_copy.wait()
    w_peak = jnp.max(jnp.abs(w_buf[...]).astype(f32))
    for c in g_copies:
        c.wait_recv()
    g_peak = jnp.max(jnp.abs(gbuf[...]).astype(f32))
    peak[0] = jnp.full(peak.shape[1:], 1.0, f32) * jnp.maximum(w_peak * g_peak, 1e-30)
    peak_copies = spread(peak, peak_send, peak_recv, row_peers)
    for c in peak_copies:
        c.start()
    ag_step(3)

    for r in range(n_row):
        block = lax.rem(row + (n_row - r), n_row)
        slot = lax.rem(col + n_col - block // 2, n_col)
        which = lax.rem(block, 2)
        gmain[r] = gbuf[slot, 0, which]
        gtail[r] = gbuf[slot, 1, which]

    g_main = gmain[...].reshape(n_row * ROWS, feats)
    g_tail = gtail[...].reshape(n_row * ROWS, feats)
    owner = lax.rem(lax.broadcasted_iota(jnp.int32, g_tail.shape, 0), ROWS) // extra
    g_quarter = [jnp.where(owner == q, g_tail, jnp.zeros_like(g_tail)) for q in range(QUARTERS)]
    tile = 256
    over_feats = (((1,), (1,)), ((), ()))

    def main_tile(t, _):
        at = pl.ds(pl.multiple_of(t * tile, tile), tile)
        res = lax.dot_general(g_main, w_buf[at, :], over_feats, preferred_element_type=f32)
        part[:, :, at] = res.reshape(n_row, ROWS, tile)
        return 0

    lax.fori_loop(0, hidden // tile, main_tile, 0)
    for t in range(quarter // tile):
        res = None
        for q in range(QUARTERS):
            term = lax.dot_general(
                g_quarter[q], w_buf[pl.ds(q * quarter + t * tile, tile), :], over_feats,
                preferred_element_type=f32,
            )
            res = term if res is None else res + term
        part[:, :, pl.ds(hidden + t * tile, tile)] = res.reshape(n_row, ROWS, tile)

    ag_step(4)
    for c in peak_copies:
        c.wait_recv()
    top = jnp.max(peak[...])
    reach = float(n_row * feats)
    scale = (2.0 ** 30 / reach) / top
    unscale = top * (reach / 2.0 ** 30)

    def rs_step(s):
        for way, p in flows:
            k = s - (half - hops(way, p))
            if 1 <= k <= hops(way, p):
                d = hops(way, p) - k + 1
                r = (n_row - d) if way == 0 else d
                v = part[r, :, lanes(p)] * scale
                if k >= 2:
                    rs_copy(way, p, k - 1).wait_recv()
                    v = v + decode(rs_in[way, p, k - 2])
                rs_out[way, p, k - 1] = encode(v)
                rs_copy(way, p, k).start()

    for h in range(5, half + 2):
        ag_step(h)
        rs_step(h - LAG)

    total = None
    over_tokens = (((0,), (0,)), ((), ()))
    a_tail = acts[:, :, pl.ds(hidden, quarter)].reshape(n_row * ROWS, quarter)
    tile_q = quarter // 3
    square = jnp.zeros((8, 128), f32)
    for q in range(QUARTERS):
        for t in range(3):
            at = q * quarter + t * tile_q
            a = acts[:, :, pl.ds(at, tile_q)].reshape(n_row * ROWS, tile_q)
            res = lax.dot_general(a, g_main, over_tokens, preferred_element_type=f32)
            res = res + lax.dot_general(
                a_tail[:, t * tile_q:(t + 1) * tile_q], g_quarter[q], over_tokens,
                preferred_element_type=f32,
            )
            raw[pl.ds(at, tile_q), :] = res
            sq = jnp.sum((res * res).reshape(tile_q // 8, 8, feats), axis=0)
            square = square + (sq[:, :128] + sq[:, 128:256] + sq[:, 256:384])
    ss_row[0] = square
    row_copies = spread(ss_row, ssr_send, ssr_recv, row_peers)
    for c in row_copies:
        c.start()
    first = half + 2 - LAG
    rs_step(first)
    for c in row_copies:
        c.wait_recv()
    ss_col[0] = jnp.sum(ss_row[...], axis=0)
    col_copies = spread(ss_col, ssc_send, ssc_recv, col_peers)
    for c in col_copies:
        c.start()
    rs_step(first + 1)
    for c in col_copies:
        c.wait_recv()
    ss_sec[0] = jnp.sum(ss_col[...], axis=0)
    sec_copies = spread(ss_sec, sss_send, sss_recv, sec_peers)
    for c in sec_copies:
        c.start()
    for s in range(first + 2, half):
        rs_step(s)
    for c in sec_copies:
        c.wait_recv()
    rs_step(half)
    sum_squares = jnp.sum(jnp.sum(ss_sec[...], axis=0), keepdims=True)
    factor = norm_target / jnp.sqrt(sum_squares + tiny_eps)

    out_copies = []
    n_out = 4
    size = hidden // n_out
    for t in range(n_out):
        at = pl.ds(t * size, size)
        out_buf[at, :] = (raw[at, :] * factor).astype(bf16)
        c = pltpu.make_async_copy(out_buf.at[at, :], gw_hbm.at[0, at, :], out_sem.at[t])
        c.start()
        out_copies.append(c)

    for p in range(PARTS):
        arrived = None
        for way in range(2):
            h = hops(way, p)
            rs_copy(way, p, h).wait_recv()
            v = decode(rs_in[way, p, h - 1])
            arrived = v if arrived is None else arrived + v
        act_grad = part[0, :, lanes(p)] + arrived * unscale
        packed[:, lanes(p)] = act_grad * slopes_buf[:, lanes(p)]
    gp_ref[0, pl.ds(0, ROWS), :] = packed[:, pl.ds(0, hidden)].astype(bf16)
    for q in range(QUARTERS):
        gp_ref[0, pl.ds(ROWS, extra), pl.ds(q * quarter, quarter)] = packed[
            pl.ds(q * extra, extra), pl.ds(hidden, quarter)
        ].astype(bf16)

    for way, p in flows:
        for h in range(1, hops(way, p) + 1):
            ag_copy(way, p, h).wait_send()
            rs_copy(way, p, h).wait_send()
    for copies in (g_copies, peak_copies, row_copies, col_copies, sec_copies):
        for c in copies:
            c.wait_send()
    for c in out_copies:
        c.wait()


def on_device(sizes, grad_out, pre_act, w_down):
    n_sec, n_row, n_col = sizes
    f32, bf16 = jnp.float32, jnp.bfloat16
    _, hidden, feats = w_down.shape
    quarter = hidden // QUARTERS
    width = hidden + quarter
    half = n_row // 2
    norm_target = target_rms * math.sqrt(float(n_sec * hidden * n_col * feats * n_row))
    dma = pltpu.SemaphoreType.DMA
    ring = (2, PARTS, half)
    vmem = pl.BlockSpec(memory_space=pltpu.VMEM)
    hbm = pl.BlockSpec(memory_space=pl.ANY)
    return pl.pallas_call(
        functools.partial(kernel, n_row, n_col, n_sec, norm_target),
        out_shape=(
            jax.ShapeDtypeStruct(pre_act.shape, bf16),
            jax.ShapeDtypeStruct(w_down.shape, bf16),
        ),
        in_specs=[vmem, vmem, hbm],
        out_specs=(vmem, hbm),
        scratch_shapes=[
            pltpu.VMEM((hidden, feats), bf16),
            pltpu.VMEM((n_row, ROWS, width), bf16),
            pltpu.VMEM((ROWS, width), f32),
            pltpu.VMEM((ROWS, width), f32),
            pltpu.VMEM((n_col, 2, 2, ROWS, feats), bf16),
            pltpu.VMEM((n_row, ROWS, feats), bf16),
            pltpu.VMEM((n_row, ROWS, feats), bf16),
            pltpu.VMEM((n_row, ROWS, width), f32),
            pltpu.VMEM((hidden, feats), f32),
            pltpu.VMEM((hidden, feats), bf16),
            pltpu.VMEM(ring + (ROWS, width // PARTS), bf16),
            pltpu.VMEM(ring + (ROWS, width // PARTS), bf16),
            pltpu.VMEM((n_row, 8, 128), f32),
            pltpu.VMEM((n_row, 8, 128), f32),
            pltpu.VMEM((n_col, 8, 128), f32),
            pltpu.VMEM((n_sec, 8, 128), f32),
            dma, dma((4,)),
            dma(ring), dma(ring), dma(ring), dma(ring),
            dma((n_col,)), dma((n_col,)),
            dma((n_row,)), dma((n_row,)),
            dma((n_row,)), dma((n_row,)),
            dma((n_col,)), dma((n_col,)),
            dma((n_sec,)), dma((n_sec,)),
        ],
        compiler_params=pltpu.CompilerParams(
            collective_id=0, has_side_effects=True, vmem_limit_bytes=56 * 1024 * 1024
        ),
        cost_estimate=pl.CostEstimate(
            flops=4 * 320 * hidden * feats, bytes_accessed=4 * hidden * feats, transcendentals=0
        ),
    )(grad_out, pre_act, w_down)


def solution(mesh):
    sizes = (mesh.shape["section"], mesh.shape["row"], mesh.shape["col"])
    in_specs = (P("section", "col", "row"), P("section", "row", "col"), P("section", "col", "row"))
    out_specs = (P("section", "row", "col"), P("section", "col", "row"))
    return jax.shard_map(
        functools.partial(on_device, sizes), mesh=mesh, in_specs=in_specs, out_specs=out_specs,
        check_vma=False,
    )
```

time: 333 us -> 87.7 us (0.26)
  blocking collectives: 189 us -> 0 us
  waiting for transfers between devices: 87.6 us -> 0 us
  Pallas kernels: 0 us -> 82 us
  between operations: 15.4 us -> 0.64 us
  local copies, waits for them, and re-layouts: 16.3 us -> 4.89 us
  matrix products: 9.23 us -> 0 us
  starting transfers between devices: 7.86 us -> 0 us
  other arithmetic: 6.12 us -> 0 us
    psum x1 -> x0, blocking collectives: 110 us -> none  [on_device(): lax.psum(jnp.sum(weight_grad * weight_grad), ('section', 'row', 'col'))]
    pallas_call x0 -> x1, Pallas kernels: none -> 82 us  [on_device(): pl.pallas_call(functools.partial(kernel, n_row, n_col, n_sec, norm_target...]
    all_gather x1 -> x0, waiting for transfers between devices: 80.7 us -> none  [on_device(): lax.all_gather(values.astype(jnp.bfloat16), 'row', axis=0, tiled=True)]
    unnamed x1 -> x0, blocking collectives: 58.9 us -> none
    all_gather x1 -> x0, blocking collectives: 19.9 us -> none  [on_device(): grad_rows = lax.all_gather(grad_block, 'col', axis=0, tiled=True)]
    unnamed x6 -> x2, local copies, waits for them, and re-layouts: 16.3 us -> 4.89 us
    dot_general x2 -> x0, matrix products: 9.23 us -> none  [the longest x1 6.14 us: on_device(): lax.dot_general(lax.all_gather(values.astype(jnp.bfloat16), 'row', axis=0...]
    unnamed x3 -> x0, starting transfers between devices: 7.83 us -> none
  transfers between devices with their start and end apart: 4 -> 0, of which waited for: 2 -> 0; matrix products, arithmetic and copies ran while one was open for 1% -> 0% of each run, Pallas kernels for 0% -> 0%
where the time goes in v1:
time: 87.7 us; the launch traced here: 87.5 us
  Pallas kernels  82 us (94%)
  local copies, waits for them, and re-layouts  4.89 us (6%)
    pallas_call x1, Pallas kernels, on_device(): pl.pallas_call(functools.partial(kernel, n_row, n_col, n_sec, norm_target...  82 us
    unnamed x2, local copies, waits for them, and re-layouts  4.89 us

profile of v1, /device:TPU:1, one launch (start us, length us, event | category | flops | bytes accessed | tf_op | source)
XLA Modules:
  0.0 87.5 jit_solution(17246055570636339867)
XLA Ops:
  0.6 82.0 %shard_map.50 = (bf16[1,20,3072]{2,1,0:T(8,128)(2,1)}, bf16[1,3072,384]{2,1,0:T(8,128)(2,1)}) custom-call(bf16[1,40,384]{2,1,0:T(8,128)(2,1)} %g_ref.1, bf16[1,20,3072]{2,1,0:T(8,128)(2,1)} %pre_ref.1, bf16[1,3072,384]{2,1,0:T(8,128)(2,1)} %w_hbm.1), custom_call_target="tpu_custom_call" | custom-call | flops 1509949440 | bytes 4718592 | tf_op jit(solution)/shard_map/pallas_call | solution.py:305
  82.7 1.6 %copy.7 = bf16[1,20,3072]{2,1,0:T(8,128)(2,1)} copy(bf16[1,20,3072]{2,1,0:T(8,128)(2,1)} %get-tuple-element.4) | data formatting | bytes 245760
  84.2 3.3 %copy.8 = bf16[1,3072,384]{2,1,0:T(8,128)(2,1)} copy(bf16[1,3072,384]{2,1,0:T(8,128)(2,1)} %get-tuple-element.5) | data formatting | bytes 4718592

commit v2 on v0

v2 whole, which is shorter than its diff:
```python
import functools
import math

import jax
import jax.numpy as jnp
from jax import lax
from jax.experimental import pallas as pl
from jax.experimental.pallas import tpu as pltpu
from jax.sharding import PartitionSpec as P

MESH = pl.DeviceIdType.MESH

gelu_coef = 0.7978845608028654
cubic_coef = 0.044715
target_rms = 0.5
tiny_eps = 1e-06

ROWS = 16
QUARTERS = 4
AG_PARTS = 3
RS_PARTS = 3
ORDER = (
    "ag1", "send_g", "ag2", "bound_w", "ag3", "wait_g", "order_g",
    "bound_g", "sums_main", "ag4", "sums_tail", "rs1", "ag5", "ag6",
    "rs2", "ag7", "rs3", "ag8", "rs4", "ag9", "weight_grad",
    "send_squares", "rs5", "rs6", "row_sums", "rs7", "col_sums", "rs8",
    "finish_factor", "grad_pre",
)


def gelu_parts(field):
    tanh_val = jnp.tanh(gelu_coef * (field + cubic_coef * field * field * field))
    values = 0.5 * field * (1.0 + tanh_val)
    slopes = 0.5 * (1.0 + tanh_val) + 0.5 * field * (1.0 - tanh_val * tanh_val) * gelu_coef * (
        1.0 + 3.0 * cubic_coef * field * field
    )
    return (values, slopes)


def encode(v):
    return (v * jnp.abs(v) * (v * v)).astype(jnp.bfloat16)


def decode(code):
    y = code.astype(jnp.float32)
    inverse = lax.rsqrt(jnp.maximum(jnp.abs(y), 2.0 ** -120))
    return (y * inverse) * (inverse * lax.rsqrt(inverse))


def kernel(
    n_row, n_col, n_sec, norm_target,
    g_hbm, pre_hbm, w_hbm, gp_ref, raw, factor_ref,
    g_ref, pre_ref,
    w_buf, acts, packed, slopes_buf, gbuf, gmain, gtail, part,
    lead_out, lead_in, rs_out, rs_in, bounds, ss_row, ss_col, ss_sec,
    in_sem, w_sem, ag_send, ag_recv, lead_send, lead_recv, rs_send, rs_recv, g_sem, sr_sem, sc_sem, ss_sem,
):
    f32, bf16 = jnp.float32, jnp.bfloat16
    row, col, sec = lax.axis_index("row"), lax.axis_index("col"), lax.axis_index("section")
    hidden, feats = w_buf.shape
    quarter = hidden // QUARTERS
    width = hidden + quarter
    extra = pre_ref.shape[1] - ROWS
    half = n_row // 2

    def peer(axis, index, size, d):
        return {axis: lax.rem(index + d, size)}

    row_peers = [peer("row", row, n_row, d) for d in range(n_row)]
    col_peers = [peer("col", col, n_col, d) for d in range(n_col)]
    sec_peers = [peer("section", sec, n_sec, d) for d in range(n_sec)]

    barrier = pltpu.get_barrier_semaphore()
    others = [row_peers[1], row_peers[n_row - 1]] + col_peers[1:] + sec_peers[1:]
    for device in others:
        pl.semaphore_signal(barrier, inc=1, device_id=device, device_id_type=MESH)
    w_copy = pltpu.make_async_copy(w_hbm.at[0], w_buf, w_sem)
    in_copies = [
        pltpu.make_async_copy(pre_hbm, pre_ref, in_sem.at[0]),
        pltpu.make_async_copy(g_hbm, g_ref, in_sem.at[1]),
    ]
    for c in in_copies:
        c.start()
    w_copy.start()
    for c in in_copies:
        c.wait()

    pre = pre_ref[0].astype(f32)
    packed[:, pl.ds(0, hidden)] = pre[:ROWS]
    for q in range(QUARTERS):
        packed[pl.ds(q * extra, extra), pl.ds(hidden, quarter)] = pre[ROWS:, q * quarter:(q + 1) * quarter]
    values, slopes = gelu_parts(packed[...])
    acts[0] = values.astype(bf16)
    slopes_buf[...] = slopes

    g = g_ref[0].astype(f32)
    for b in range(2):
        base = b * (ROWS + extra)
        gbuf[0, 0, b] = g[base:base + ROWS].astype(bf16)
        last = g[base + ROWS:base + ROWS + extra]
        gbuf[0, 1, b] = jnp.concatenate([last] * QUARTERS, axis=0).astype(bf16)

    pl.semaphore_wait(barrier, len(others))

    def flows(parts):
        return [(way, p) for p in range(parts) for way in range(2)]

    def hops(way, p):
        return half if (way + p) % 2 == 0 else half - 1

    def lanes(p, parts):
        return pl.ds(p * (width // parts), width // parts)

    def places(parts, lead):
        keys = [
            (way, p, j) for way, p in flows(parts) for j in range(1, hops(way, p) + 1)
            if not (lead and p == way)
        ]
        return {key: i for i, key in enumerate(keys)}

    ag_place, rs_place = places(AG_PARTS, False), places(RS_PARTS, True)

    def onward(way):
        return row_peers[1 if way == 0 else n_row - 1]

    def ag_copy(way, p, j):
        src, dst = (j - 1, j) if way == 0 else ((n_row - j + 1) % n_row, n_row - j)
        at = lanes(p, AG_PARTS)
        return pltpu.make_async_remote_copy(
            src_ref=acts.at[src, :, at], dst_ref=acts.at[dst, :, at],
            send_sem=ag_send, recv_sem=ag_recv.at[ag_place[way, p, j]],
            device_id=onward(way), device_id_type=MESH,
        )

    def rs_slot(way, p, j, out):
        if p == way:
            return (lead_out if out else lead_in).at[way * half + j - 1]
        return (rs_out if out else rs_in).at[rs_place[way, p, j]]

    def rs_copy(way, p, j):
        lead = p == way
        return pltpu.make_async_remote_copy(
            src_ref=rs_slot(way, p, j, True), dst_ref=rs_slot(way, p, j, False),
            send_sem=lead_send if lead else rs_send,
            recv_sem=lead_recv.at[way * half + j - 1] if lead else rs_recv.at[rs_place[way, p, j]],
            device_id=onward(way), device_id_type=MESH,
        )

    def spread(buf, sems, peers):
        for d in range(1, len(peers)):
            pltpu.make_async_remote_copy(
                src_ref=buf.at[0], dst_ref=buf.at[d], send_sem=sems.at[0], recv_sem=sems.at[1],
                device_id=peers[d], device_id_type=MESH,
            ).start()

    def whole(buf, send_sem, recv_sem, count):
        every = buf.at[pl.ds(buf.shape[0] - count, count)]
        return pltpu.make_async_remote_copy(
            src_ref=every, dst_ref=every, send_sem=send_sem, recv_sem=recv_sem,
            device_id=row_peers[1], device_id_type=MESH,
        )

    def gathered(buf, sems):
        whole(buf, sems.at[0], sems.at[1], buf.shape[0] - 1).wait_recv()

    def ag_part(h, way, p):
        if 1 <= h - 1 <= hops(way, p):
            ag_copy(way, p, h - 1).wait_recv()
        if h <= hops(way, p):
            ag_copy(way, p, h).start()

    def ag_step(h):
        for way, p in flows(AG_PARTS):
            ag_part(h, way, p)

    over_feats = (((1,), (1,)), ((), ()))
    over_tokens = (((0,), (0,)), ((), ()))
    def order_g():
        for r in range(n_row):
            block = lax.rem(row + (n_row - r), n_row)
            slot = lax.rem(col + n_col - block // 2, n_col)
            which = lax.rem(block, 2)
            gmain[r] = gbuf[slot, 0, which]
            gtail[r] = gbuf[slot, 1, which]

    def g_blocks():
        g_main = gmain[...].reshape(n_row * ROWS, feats)
        g_tail = gtail[...].reshape(n_row * ROWS, feats)
        owner = lax.rem(lax.broadcasted_iota(jnp.int32, g_tail.shape, 0), ROWS) // extra
        return g_main, [jnp.where(owner == q, g_tail, jnp.zeros_like(g_tail)) for q in range(QUARTERS)]

    tile = 256

    def sums_main():
        g_main, _ = g_blocks()

        def main_tile(t, _):
            at = pl.ds(pl.multiple_of(t * tile, tile), tile)
            res = lax.dot_general(g_main, w_buf[at, :], over_feats, preferred_element_type=f32)
            part[:, :, at] = res.reshape(n_row, ROWS, tile)
            return 0

        lax.fori_loop(0, hidden // tile, main_tile, 0)

    def sums_tail():
        _, g_quarter = g_blocks()
        for t in range(quarter // tile):
            res = None
            for q in range(QUARTERS):
                term = lax.dot_general(
                    g_quarter[q], w_buf[pl.ds(q * quarter + t * tile, tile), :], over_feats,
                    preferred_element_type=f32,
                )
                res = term if res is None else res + term
            part[:, :, pl.ds(hidden + t * tile, tile)] = res.reshape(n_row, ROWS, tile)

    def bound_w():
        w_copy.wait()
        bounds[0] = jnp.full(bounds.shape[1:], jnp.max(jnp.abs(w_buf[...]).astype(f32)))

    def bound_g():
        top = bounds[0] * (jnp.max(jnp.abs(gbuf[...]).astype(f32)) * feats)
        bounds[0] = jnp.maximum(top, 1e-30)

    one = 2.0 ** 27
    pw = width // RS_PARTS

    def wide(block):
        return jnp.concatenate([block] * (pw // 128), axis=1)

    def received(way, p, j):
        return decode(rs_slot(way, p, j, False)[:, pl.ds(0, pw)])

    def bound_in(way, j):
        return rs_slot(way, way, j, False)[:, pl.ds(pw, 128)].astype(f32)

    def parts_of(way):
        return [way] + [p for p in range(RS_PARTS) if p != way]

    scales = {}

    def rs_part(s, way, p):
        j = half + 1 - s
        if j > hops(way, p):
            return
        if j < hops(way, p):
            rs_copy(way, p, j + 1).wait_recv()
        if p == way:
            bound = bounds[0]
            back = None
            if j < half:
                into = bound_in(way, j + 1)
                bound = jnp.maximum(bound, into)
                back = wide(into * (1.0 / one))
            bound = bound.astype(bf16)
            rs_slot(way, p, j, True)[:, pl.ds(pw, 128)] = bound
            scales[way] = wide(one / bound.astype(f32)), back
        scale, back = scales[way]
        v = part[(n_row - j) if way == 0 else j, :, lanes(p, RS_PARTS)]
        if j < hops(way, p):
            v = v + received(way, p, j + 1) * back
        rs_slot(way, p, j, True)[:, pl.ds(0, pw)] = encode(v * scale)
        rs_copy(way, p, j).start()

    def rs_step(s):
        for i in range(RS_PARTS):
            for way in range(2):
                rs_part(s, way, parts_of(way)[i])

    def weight_grad():
        g_main, g_quarter = g_blocks()
        a_tail = acts[:, :, pl.ds(hidden, quarter)].reshape(n_row * ROWS, quarter)
        size = quarter // 3
        square = jnp.zeros((8, 128), f32)
        for q in range(QUARTERS):
            for t in range(3):
                at = q * quarter + t * size
                a = acts[:, :, pl.ds(at, size)].reshape(n_row * ROWS, size)
                res = lax.dot_general(a, g_main, over_tokens, preferred_element_type=f32)
                res = res + lax.dot_general(
                    a_tail[:, t * size:(t + 1) * size], g_quarter[q], over_tokens,
                    preferred_element_type=f32,
                )
                raw[pl.ds(at, size), :] = res
                sq = jnp.sum((res * res).reshape(size // 8, 8, feats), axis=0)
                for c in range(feats // 128):
                    square = square + sq[:, c * 128:(c + 1) * 128]
        ss_row[0] = square

    def finish_factor():
        gathered(ss_sec, ss_sem)
        sum_squares = jnp.sum(jnp.sum(ss_sec[...], axis=0), keepdims=True)
        factor_ref[...] = jnp.broadcast_to(norm_target / jnp.sqrt(sum_squares + tiny_eps), (8, 128))

    def grad_pre():
        back = []
        for way in range(2):
            rs_copy(way, way, 1).wait_recv()
            back.append(wide(bound_in(way, 1) * (1.0 / one)))
        for p in range(RS_PARTS):
            at = lanes(p, RS_PARTS)
            act_grad = part[0, :, at]
            for way in range(2):
                if p != way:
                    rs_copy(way, p, 1).wait_recv()
                act_grad = act_grad + received(way, p, 1) * back[way]
            packed[:, at] = act_grad * slopes_buf[:, at]
        gp_ref[0, pl.ds(0, ROWS), :] = packed[:, pl.ds(0, hidden)].astype(bf16)
        for q in range(QUARTERS):
            gp_ref[0, pl.ds(ROWS, extra), pl.ds(q * quarter, quarter)] = packed[
                pl.ds(q * extra, extra), pl.ds(hidden, quarter)
            ].astype(bf16)

    def row_sums():
        gathered(ss_row, sr_sem)
        ss_col[0] = jnp.sum(ss_row[...], axis=0)
        spread(ss_col, sc_sem, col_peers)

    def col_sums():
        gathered(ss_col, sc_sem)
        ss_sec[0] = jnp.sum(ss_col[...], axis=0)
        spread(ss_sec, ss_sem, sec_peers)

    steps = dict(
        bound_w=bound_w,
        bound_g=bound_g,
        send_g=lambda: spread(gbuf, g_sem, col_peers),
        wait_g=lambda: gathered(gbuf, g_sem),
        order_g=order_g,
        sums_main=sums_main,
        sums_tail=sums_tail,
        weight_grad=weight_grad,
        send_squares=lambda: spread(ss_row, sr_sem, row_peers),
        row_sums=row_sums,
        col_sums=col_sums,
        finish_factor=finish_factor,
        grad_pre=grad_pre,
    )
    for h in range(1, half + 2):
        steps["ag%d" % h] = functools.partial(ag_step, h)
        steps["rs%d" % h] = functools.partial(rs_step, h)
    for name in ORDER:
        steps[name]()

    whole(acts, ag_send, ag_recv.at[0], n_row - 1).wait_send()
    whole(lead_out, lead_send, lead_recv.at[0], lead_out.shape[0]).wait_send()
    whole(rs_out, rs_send, rs_recv.at[0], rs_out.shape[0]).wait_send()
    for buf, sems in (
        (gbuf, g_sem), (ss_row, sr_sem), (ss_col, sc_sem), (ss_sec, ss_sem),
    ):
        whole(buf, sems.at[0], sems.at[1], buf.shape[0] - 1).wait_send()


def scale_kernel(n_out, raw, factor_ref, gp_ref, gw_hbm, gp_hbm, out_buf, sems):
    gp_copy = pltpu.make_async_copy(gp_ref, gp_hbm, sems.at[n_out])
    gp_copy.start()
    factor = factor_ref[0:1, 0:1]
    size = raw.shape[0] // n_out
    copies = []
    for t in range(n_out):
        at = pl.ds(t * size, size)
        out_buf[at, :] = (raw[at, :] * factor).astype(jnp.bfloat16)
        c = pltpu.make_async_copy(out_buf.at[at, :], gw_hbm.at[0, at, :], sems.at[t])
        c.start()
        copies.append(c)
    for c in copies:
        c.wait()
    gp_copy.wait()


def on_device(sizes, grad_out, pre_act, w_down):
    n_sec, n_row, n_col = sizes
    f32, bf16 = jnp.float32, jnp.bfloat16
    _, hidden, feats = w_down.shape
    width = hidden + hidden // QUARTERS
    norm_target = target_rms * math.sqrt(float(n_sec * hidden * n_col * feats * n_row))
    dma = pltpu.SemaphoreType.DMA
    n_ag, n_rs = AG_PARTS * (n_row - 1), RS_PARTS * (n_row - 1) - n_row
    vmem = pl.BlockSpec(memory_space=pltpu.VMEM)
    hbm = pl.BlockSpec(memory_space=pl.ANY)
    small = (8, 128)
    gp, raw, factor = pl.pallas_call(
        functools.partial(kernel, n_row, n_col, n_sec, norm_target),
        out_shape=(
            pltpu.VMEM(pre_act.shape, bf16),
            pltpu.VMEM((hidden, feats), f32),
            pltpu.VMEM(small, f32),
        ),
        in_specs=[hbm, hbm, hbm],
        out_specs=(vmem, vmem, vmem),
        scratch_shapes=[
            pltpu.VMEM(grad_out.shape, bf16),
            pltpu.VMEM(pre_act.shape, bf16),
            pltpu.VMEM((hidden, feats), bf16),
            pltpu.VMEM((n_row, ROWS, width), bf16),
            pltpu.VMEM((ROWS, width), f32),
            pltpu.VMEM((ROWS, width), f32),
            pltpu.VMEM((n_col, 2, 2, ROWS, feats), bf16),
            pltpu.VMEM((n_row, ROWS, feats), bf16),
            pltpu.VMEM((n_row, ROWS, feats), bf16),
            pltpu.VMEM((n_row, ROWS, width), f32),
            pltpu.VMEM((n_row, ROWS, width // RS_PARTS + 128), bf16),
            pltpu.VMEM((n_row, ROWS, width // RS_PARTS + 128), bf16),
            pltpu.VMEM((n_rs, ROWS, width // RS_PARTS), bf16),
            pltpu.VMEM((n_rs, ROWS, width // RS_PARTS), bf16),
            pltpu.VMEM((1, ROWS, 128), f32),
            pltpu.VMEM((n_row,) + small, f32),
            pltpu.VMEM((n_col,) + small, f32),
            pltpu.VMEM((n_sec,) + small, f32),
            dma((2,)), dma, dma, dma((n_ag,)), dma, dma((n_row,)), dma, dma((n_rs,)),
            dma((2,)), dma((2,)), dma((2,)), dma((2,)),
        ],
        compiler_params=pltpu.CompilerParams(
            collective_id=0, has_side_effects=True, vmem_limit_bytes=58 * 1024 * 1024
        ),
        cost_estimate=pl.CostEstimate(
            flops=4 * 320 * hidden * feats, bytes_accessed=4 * hidden * feats, transcendentals=0
        ),
    )(grad_out, pre_act, w_down)
    n_out = 4
    gw, gp = pl.pallas_call(
        functools.partial(scale_kernel, n_out),
        out_shape=(
            jax.ShapeDtypeStruct(w_down.shape, bf16),
            jax.ShapeDtypeStruct(pre_act.shape, bf16),
        ),
        in_specs=[vmem, vmem, vmem],
        out_specs=(hbm, hbm),
        scratch_shapes=[pltpu.VMEM((hidden, feats), bf16), dma((n_out + 1,))],
        compiler_params=pltpu.CompilerParams(vmem_limit_bytes=16 * 1024 * 1024),
    )(raw, factor, gp)
    return gp, gw


def solution(mesh):
    sizes = (mesh.shape["section"], mesh.shape["row"], mesh.shape["col"])
    in_specs = (P("section", "col", "row"), P("section", "row", "col"), P("section", "col", "row"))
    out_specs = (P("section", "row", "col"), P("section", "col", "row"))
    return jax.shard_map(
        functools.partial(on_device, sizes), mesh=mesh, in_specs=in_specs, out_specs=out_specs,
        check_vma=False,
    )
```

time: 333 us -> 70.7 us (0.21)
  blocking collectives: 189 us -> 0 us
  waiting for transfers between devices: 87.6 us -> 0 us
  Pallas kernels: 0 us -> 69.9 us
  local copies, waits for them, and re-layouts: 16.3 us -> 0 us
  between operations: 15.4 us -> 0.64 us
  matrix products: 9.23 us -> 0 us
  starting transfers between devices: 7.86 us -> 0 us
  other arithmetic: 6.12 us -> 0 us
    psum x1 -> x0, blocking collectives: 110 us -> none  [on_device(): lax.psum(jnp.sum(weight_grad * weight_grad), ('section', 'row', 'col'))]
    all_gather x1 -> x0, waiting for transfers between devices: 80.7 us -> none  [on_device(): lax.all_gather(values.astype(jnp.bfloat16), 'row', axis=0, tiled=True)]
    pallas_call x0 -> x2, Pallas kernels: none -> 69.9 us  [the longest x1 68.3 us: on_device(): pl.pallas_call(functools.partial(kernel, n_row, n_col, n_sec, norm_target...]
    unnamed x1 -> x0, blocking collectives: 58.9 us -> none
    all_gather x1 -> x0, blocking collectives: 19.9 us -> none  [on_device(): grad_rows = lax.all_gather(grad_block, 'col', axis=0, tiled=True)]
    unnamed x6 -> x0, local copies, waits for them, and re-layouts: 16.3 us -> none
    dot_general x2 -> x0, matrix products: 9.23 us -> none  [the longest x1 6.14 us: on_device(): lax.dot_general(lax.all_gather(values.astype(jnp.bfloat16), 'row', axis=0...]
    unnamed x3 -> x0, starting transfers between devices: 7.83 us -> none
  transfers between devices with their start and end apart: 4 -> 0, of which waited for: 2 -> 0; matrix products, arithmetic and copies ran while one was open for 1% -> 0% of each run, Pallas kernels for 0% -> 0%
where the time goes in v2:
time: 70.7 us; the launch traced here: 70.5 us
  Pallas kernels  69.9 us (99%)
    pallas_call x1, Pallas kernels, on_device(): pl.pallas_call(functools.partial(kernel, n_row, n_col, n_sec, norm_target...  68.3 us
    pallas_call x1, Pallas kernels, on_device(): pl.pallas_call(functools.partial(scale_kernel, n_out), out_shape=(jax.Sha...  1.61 us

profile of v2, /device:TPU:1, one launch (start us, length us, event | category | flops | bytes accessed | tf_op | source)
XLA Modules:
  0.0 70.5 jit_solution(10441794824527699588)
XLA Ops:
  0.6 68.3 %shard_map.50 = (bf16[1,20,3072]{2,1,0:T(8,128)(2,1)S(1)}, f32[3072,384]{1,0:T(8,128)S(1)}, f32[8,128]{1,0:T(8,128)S(1)}) custom-call(bf16[1,40,384]{2,1,0:T(8,128)(2,1)} %g_hbm.1, bf16[1,20,3072]{2,1,0:T(8,128)(2,1)} %pre_hbm.1, bf16[1,3072,384]{2,1,0:T(8,128)(2,1)} %w_hbm.1), custom_call_target="tpu_custom_call" | custom-call | flops 1509949440 | bytes 4718592 | tf_op jit(solution)/shard_map/pallas_call | solution.py:382
  68.9 1.6 %shard_map.51 = (bf16[1,3072,384]{2,1,0:T(8,128)(2,1)}, bf16[1,20,3072]{2,1,0:T(8,128)(2,1)}) custom-call(f32[3072,384]{1,0:T(8,128)S(1)} %get-tuple-element.7.raw, f32[8,128]{1,0:T(8,128)S(1)} %get-tuple-element.8.factor_ref, bf16[1,20,3072]{2,1,0:T(8,128)(2,1)S(1)} %get-tuple-element.9.gp_ref), custom_call_target="tpu_custom_call" | custom-call | tf_op jit(solution)/shard_map/pallas_call | solution.py:421

commit v3 on v2

--- a/solution.py
+++ b/solution.py
@@ -20,21 +20,27 @@
 AG_PARTS = 3
 RS_PARTS = 3
 ORDER = (
-    "ag1", "send_g", "ag2", "bound_w", "ag3", "wait_g", "order_g",
-    "bound_g", "sums_main", "ag4", "sums_tail", "rs1", "ag5", "ag6",
-    "rs2", "ag7", "rs3", "ag8", "rs4", "ag9", "weight_grad",
-    "send_squares", "rs5", "rs6", "row_sums", "rs7", "col_sums", "rs8",
-    "finish_factor", "grad_pre",
+    "ag1", "send_g", "slopes", "ag2", "bound_w", "ag3", "wait_g",
+    "order_g", "bound_g", "sums_main", "ag4", "sums_tail", "rs1", "ag5",
+    "ag6", "rs2", "ag7", "rs3", "ag8", "rs4", "ag9",
+    "weight_grad", "send_squares", "rs5", "rs6", "row_sums", "rs7", "rs8",
+    "col_sums", "grad_pre", "finish_factor",
 )
 
 
-def gelu_parts(field):
-    tanh_val = jnp.tanh(gelu_coef * (field + cubic_coef * field * field * field))
-    values = 0.5 * field * (1.0 + tanh_val)
-    slopes = 0.5 * (1.0 + tanh_val) + 0.5 * field * (1.0 - tanh_val * tanh_val) * gelu_coef * (
+def gelu_tanh(field):
+    return jnp.tanh(gelu_coef * (field + cubic_coef * field * field * field))
+
+
+def gelu_values(field):
+    return 0.5 * field * (1.0 + gelu_tanh(field))
+
+
+def gelu_slopes(field):
+    tanh_val = gelu_tanh(field)
+    return 0.5 * (1.0 + tanh_val) + 0.5 * field * (1.0 - tanh_val * tanh_val) * gelu_coef * (
         1.0 + 3.0 * cubic_coef * field * field
     )
-    return (values, slopes)
 
 
 def encode(v):
@@ -82,23 +88,12 @@
     for c in in_copies:
         c.start()
     w_copy.start()
-    for c in in_copies:
-        c.wait()
-
+    in_copies[0].wait()
     pre = pre_ref[0].astype(f32)
     packed[:, pl.ds(0, hidden)] = pre[:ROWS]
     for q in range(QUARTERS):
         packed[pl.ds(q * extra, extra), pl.ds(hidden, quarter)] = pre[ROWS:, q * quarter:(q + 1) * quarter]
-    values, slopes = gelu_parts(packed[...])
-    acts[0] = values.astype(bf16)
-    slopes_buf[...] = slopes
-
-    g = g_ref[0].astype(f32)
-    for b in range(2):
-        base = b * (ROWS + extra)
-        gbuf[0, 0, b] = g[base:base + ROWS].astype(bf16)
-        last = g[base + ROWS:base + ROWS + extra]
-        gbuf[0, 1, b] = jnp.concatenate([last] * QUARTERS, axis=0).astype(bf16)
+    acts[0] = gelu_values(packed[...]).astype(bf16)
 
     pl.semaphore_wait(barrier, len(others))
 
@@ -172,6 +167,19 @@
     def ag_step(h):
         for way, p in flows(AG_PARTS):
             ag_part(h, way, p)
+
+    def pack_g():
+        in_copies[1].wait()
+        g = g_ref[0].astype(f32)
+        for b in range(2):
+            base = b * (ROWS + extra)
+            gbuf[0, 0, b] = g[base:base + ROWS].astype(bf16)
+            last = g[base + ROWS:base + ROWS + extra]
+            gbuf[0, 1, b] = jnp.concatenate([last] * QUARTERS, axis=0).astype(bf16)
+        spread(gbuf, g_sem, col_peers)
+
+    def slopes():
+        slopes_buf[...] = gelu_slopes(packed[...])
 
     over_feats = (((1,), (1,)), ((), ()))
     over_tokens = (((0,), (0,)), ((), ()))
@@ -324,7 +332,8 @@
     steps = dict(
         bound_w=bound_w,
         bound_g=bound_g,
-        send_g=lambda: spread(gbuf, g_sem, col_peers),
+        send_g=pack_g,
+        slopes=slopes,
         wait_g=lambda: gathered(gbuf, g_sem),
         order_g=order_g,
         sums_main=sums_main,

time: 70.7 us -> 69.8 us (0.987); the launches traced: 70.5 us -> 68.6 us
  Pallas kernels: 69.9 us -> 67.9 us
    pallas_call x1, Pallas kernels: 68.3 us -> 66.3 us  [on_device(): pl.pallas_call(functools.partial(kernel, n_row, n_col, n_sec, norm_target...]
where the time goes in v3:
time: 69.8 us; the launch traced here: 68.6 us
  Pallas kernels  67.9 us (97%)
    pallas_call x1, Pallas kernels, on_device(): pl.pallas_call(functools.partial(kernel, n_row, n_col, n_sec, norm_target...  66.3 us
    pallas_call x1, Pallas kernels, on_device(): pl.pallas_call(functools.partial(scale_kernel, n_out), out_shape=(jax.Sha...  1.61 us

profile of v3, /device:TPU:1, one launch (start us, length us, event | category | flops | bytes accessed | tf_op | source)
XLA Modules:
  0.0 68.6 jit_solution(9108679229538594936)
XLA Ops:
  0.6 66.3 %shard_map.50 = (bf16[1,20,3072]{2,1,0:T(8,128)(2,1)S(1)}, f32[3072,384]{1,0:T(8,128)S(1)}, f32[8,128]{1,0:T(8,128)S(1)}) custom-call(bf16[1,40,384]{2,1,0:T(8,128)(2,1)} %g_hbm.1, bf16[1,20,3072]{2,1,0:T(8,128)(2,1)} %pre_hbm.1, bf16[1,3072,384]{2,1,0:T(8,128)(2,1)} %w_hbm.1), custom_call_target="tpu_custom_call" | custom-call | flops 1509949440 | bytes 4718592 | tf_op jit(solution)/shard_map/pallas_call | solution.py:391
  67.0 1.6 %shard_map.51 = (bf16[1,3072,384]{2,1,0:T(8,128)(2,1)}, bf16[1,20,3072]{2,1,0:T(8,128)(2,1)}) custom-call(f32[3072,384]{1,0:T(8,128)S(1)} %get-tuple-element.7.raw, f32[8,128]{1,0:T(8,128)S(1)} %get-tuple-element.8.factor_ref, bf16[1,20,3072]{2,1,0:T(8,128)(2,1)S(1)} %get-tuple-element.9.gp_ref), custom_call_target="tpu_custom_call" | custom-call | tf_op jit(solution)/shard_map/pallas_call | solution.py:430
